TPU v7x, 128 devices: a whole 4x4x4 slice. The times are simulated.
128 devices in a mesh: shot: 16 (over y, x_hi, core), pt: 8 (over z, x_lo).
Axes of the slice: x: 4 (x_hi: 2, x_lo: 2; x = x_hi * 2 + x_lo), y: 4, z: 4, core: 2. Of those that a mesh axis runs over, the one named last changes fastest.
Arguments:
- shot_data: bfloat16 [256, 128, 1024], P('shot', 'pt'), may hold values from -0.29882812 to 0.29882812
- point_store: bfloat16 [128, 576, 1024], P(('shot', 'pt')), may hold values from -0.29882812 to 0.29882812
- point_slot: int32 [128], P('pt'), may hold values from 0 to 127, as said below
- taper_mask: int32 [256, 128], P('shot', 'pt'), may hold values 0 or 1
- recv_start: int32 [256], P('shot'), may hold values from 0 to 64
Outputs:
- multiples: float32 [256, 512, 1024], P('shot', 'pt')
Inputs may be any that keep to these rules, and one draw needn't show every extreme that they name: `point_slot`: A permutation of the slots; the gathers of the inner points k with k // 16 = b lie in the slots q with (q) % (8) = b.
All inputs are finite; a program needn't handle non-finite values. No bound on the sum of `taper_mask` on one device may be relied on, other than what follows from the above.
Results may differ from a plain program's by a relative error of at most 0.0063.
Values may be sent and summed in bfloat16 or wider, within the bound.
No kernel may reach another device: no remote copies, remote signals or barrier semaphores. Data moves between devices by JAX's collectives and lax.ppermute only.
A program may use at most 192 MiB of HBM per device.

v0:
```python
import math

import jax
import jax.numpy as jnp
from jax import lax
from jax.sharding import PartitionSpec as P

NF = 256
SPREAD = 512


def band_tables(samples, bins):
    times_idx = jnp.arange(samples, dtype=jnp.int32)[:, None]
    freq_idx = jnp.arange(bins, dtype=jnp.int32)[None, :]
    phase_idx = times_idx * freq_idx % samples
    phase_angle = phase_idx.astype(jnp.float32) * jnp.float32(2.0 * math.pi / samples)
    cosine = jnp.cos(phase_angle)
    sine = jnp.sin(phase_angle)
    forward = jnp.concatenate([cosine, -sine], axis=1).astype(jnp.bfloat16)
    weights = jnp.where(freq_idx == 0, jnp.float32(1.0), jnp.float32(2.0)) / jnp.float32(samples)
    inverse = jnp.concatenate([(weights * cosine).T, (-weights * sine).T], axis=0).astype(
        jnp.bfloat16
    )
    return (forward, inverse)


def complex_product(left_part, right_part, bins):
    left_real = left_part[..., :bins]
    left_imag = left_part[..., bins:]
    right_real = right_part[..., :bins]
    right_imag = right_part[..., bins:]
    real_part = jnp.einsum(
        "skf,krf->srf", left_real, right_real, preferred_element_type=jnp.float32
    ) - jnp.einsum("skf,krf->srf", left_imag, right_imag, preferred_element_type=jnp.float32)
    imag_part = jnp.einsum(
        "skf,krf->srf", left_real, right_imag, preferred_element_type=jnp.float32
    ) + jnp.einsum("skf,krf->srf", left_imag, right_real, preferred_element_type=jnp.float32)
    return jnp.concatenate([real_part, imag_part], axis=-1)


def per_device(shot_data, point_store, point_slot, taper_mask, recv_start):
    inner_count = shot_data.shape[1]
    own_slots = point_store.shape[0]
    pt_count = lax.axis_size("pt")
    forward, inverse = band_tables(shot_data.shape[2], NF)
    spectra = jnp.dot(shot_data, forward, preferred_element_type=jnp.float32)
    spectra = (spectra * taper_mask[:, :, None].astype(jnp.float32)).astype(jnp.bfloat16)
    slot_of = point_slot // (own_slots * pt_count) * own_slots + point_slot % own_slots
    onehot = (slot_of[:, None] == jnp.arange(inner_count, dtype=jnp.int32)[None, :]).astype(
        jnp.bfloat16
    )
    ordered = jnp.einsum("ij,sif->sjf", onehot, spectra, preferred_element_type=jnp.float32).astype(
        jnp.bfloat16
    )
    collected = jnp.dot(
        lax.all_gather(point_store, "shot", axis=0, tiled=True),
        forward,
        preferred_element_type=jnp.float32,
    ).astype(jnp.bfloat16)
    predicted = complex_product(ordered, collected, NF)

    def window(shot_row, first_rec):
        return lax.dynamic_slice_in_dim(shot_row, first_rec, SPREAD, 0)

    windows = jax.vmap(window)(predicted, recv_start)
    rounded = lax.psum_scatter(windows, "pt", scatter_dimension=1, tiled=True).astype(jnp.bfloat16)
    return jnp.dot(rounded, inverse, preferred_element_type=jnp.float32)


def solution(mesh):
    placed = (
        P("shot", "pt", None),
        P(("shot", "pt"), None, None),
        P("pt"),
        P("shot", "pt"),
        P("shot"),
    )
    return jax.shard_map(
        per_device, mesh=mesh, in_specs=placed, out_specs=P("shot", "pt", None), check_vma=False
    )
```

profile of v0, /device:TPU:1, one launch (start us, length us, event | category | flops | bytes accessed | tf_op | source)
XLA Modules:
  0.0 686.3 jit_solution(7969781934846037813)
XLA Ops:
  6.5 0.7 all-gather.2.cloned.1.call-update
  7.3 0.7 convert_element_type.42
  8.0 4.4 negate_convert_fusion
  12.4 0.7 and_select_fusion
  13.1 0.6 fusion.1
  13.8 1.0 copy.10
  14.8 1.0 copy.7
  15.8 116.4 %all-gather.2.cloned.1.call-done = bf16[16,576,1024]{2,1,0:T(8,128)(2,1)} async-done(((bf16[1,576,1024]{2,1,0:T(8,128)(2,1)}), bf16[16,576,1024]{2,1,0:T(8,128)(2,1)}) %all-gather.2.cloned.1.call-update) | async-done | bytes 18874384 | tf_op jit(solution)/shard_map/all_gather | solution.py:56
  132.2 16.0 %convert_bitcast_fusion = bf16[16,576,512]{2,1,0:T(8,128)(2,1)} fusion(bf16[16,576,1024]{2,1,0:T(8,128)(2,1)} %all-gather.2.cloned.1.call-done, bf16[1024,256]{1,0:T(8,128)(2,1)S(1)} %get-tuple-element.27, bf16[1024,256]{1,0:T(8,128)(2,1)} %copy-done.3), kind=kOutput, calls=%fused_computation.5 | convolution fusion | flops 9670492160 | bytes 29360128 | tf_op jit(solution)/shard_map/dot_general | solution.py:55
  148.2 8.4 %fusion.31 = (bf16[16,576,256]{2,1,0:T(8,128)(2,1)}, bf16[16,576,256]{2,1,0:T(8,128)(2,1)}) fusion(bf16[16,576,512]{2,1,0:T(8,128)(2,1)} %convert_bitcast_fusion), kind=kLoop, calls=%fused_computation.57 | loop fusion | bytes 18874368 | tf_op jit(solution)/shard_map/slice | solution.py:30
  156.6 8.9 %copy.9 = bf16[16,576,256]{1,0,2:T(8,128)(2,1)} copy(bf16[16,576,256]{2,1,0:T(8,128)(2,1)} %get-tuple-element.24) | data formatting | bytes 9437184 | tf_op jit(solution)/shard_map/slice | solution.py:31
  165.5 8.9 %copy.6 = bf16[16,576,256]{1,0,2:T(8,128)(2,1)} copy(bf16[16,576,256]{2,1,0:T(8,128)(2,1)} %get-tuple-element.23) | data formatting | bytes 9437184 | tf_op jit(solution)/shard_map/slice | solution.py:30
  174.4 8.1 %fusion.34 = f32[256,576,16]{1,2,0:T(8,128)} fusion(bf16[16,576,256]{1,0,2:T(8,128)(2,1)} %copy.9, bf16[16,16,256]{0,1,2:T(8,128)(2,1)S(1)} %copy.10), kind=kOutput, calls=%fused_computation.60 | convolution fusion | flops 75497472 | bytes 14286848 | tf_op jit(solution)/shard_map/skf,krf->srf/dot_general | solution.py:34
  182.5 5.6 fusion.36
  188.1 5.6 fusion.33
  193.7 5.5 fusion.35
  199.3 10.9 %copy.11 = f32[256,576,16]{0,1,2:T(8,128)} copy(f32[256,576,16]{1,2,0:T(8,128)} %fusion.34) | data formatting | bytes 18874368 | tf_op jit(solution)/shard_map/skf,krf->srf/dot_general | solution.py:34
  210.2 10.9 %copy.8 = f32[256,576,16]{0,1,2:T(8,128)} copy(f32[256,576,16]{1,2,0:T(8,128)} %fusion.33) | data formatting | bytes 18874368 | tf_op jit(solution)/shard_map/skf,krf->srf/dot_general | solution.py:32
  221.1 10.9 %copy.13 = f32[256,576,16]{0,1,2:T(8,128)} copy(f32[256,576,16]{1,2,0:T(8,128)} %fusion.36) | data formatting | bytes 18874368 | tf_op jit(solution)/shard_map/skf,krf->srf/dot_general | solution.py:37
  232.0 10.9 %copy.12 = f32[256,576,16]{0,1,2:T(8,128)} copy(f32[256,576,16]{1,2,0:T(8,128)} %fusion.35) | data formatting | bytes 18874368 | tf_op jit(solution)/shard_map/skf,krf->srf/dot_general | solution.py:35
  242.9 11.3 %subtract_bitcast_fusion = f32[16,576,256]{2,1,0:T(8,128)} fusion(f32[256,576,16]{0,1,2:T(8,128)} %copy.8, f32[256,576,16]{0,1,2:T(8,128)} %copy.11), kind=kLoop, calls=%fused_computation.4 | loop fusion | flops 2359296 | bytes 28311552 | tf_op jit(solution)/shard_map/sub | solution.py:32
  254.3 11.6 %add_bitcast_fusion = f32[16,576,256]{2,1,0:T(8,128)} fusion(f32[256,576,16]{0,1,2:T(8,128)} %copy.12, f32[256,576,16]{0,1,2:T(8,128)} %copy.13), kind=kLoop, calls=%fused_computation.3 | loop fusion | flops 2359296 | bytes 28311552 | tf_op jit(solution)/shard_map/add | solution.py:35
  265.8 15.0 %pad_maximum_fusion = f32[16,576,512]{2,1,0:T(8,128)} fusion(f32[16,576,256]{2,1,0:T(8,128)} %add_bitcast_fusion, f32[16,576,256]{2,1,0:T(8,128)} %subtract_bitcast_fusion), kind=kLoop, calls=%fused_computation.2 | loop fusion | flops 4718592 | bytes 37748736 | tf_op jit(solution)/shard_map/concatenate | solution.py:38
  280.9 69.8 %while.1 = (s32[]{:T(128)}, f32[16,576,512]{2,1,0:T(8,128)}, s32[16,3]{0,1:T(4,128)S(1)}, f32[16,512,512]{2,1,0:T(8,128)}, s32[]{:T(128)}) while((s32[]{:T(128)}, f32[16,576,512]{2,1,0:T(8,128)}, s32[16,3]{0,1:T(4,128)S(1)}, f32[16,512,512]{2,1,0:T(8,128)}, s32[]{:T(128)}) %tuple.23), condition=%wide.while_cond, body=%wide.while_body.sunk | while | flops 2 | bytes 2098793 | solution.py:63
  280.9 0.6 fusion.48
  281.5 3.7 dynamic-slice_dynamic-update-slice_fusion.2
  285.3 0.6 fusion.48
  285.9 3.7 dynamic-slice_dynamic-update-slice_fusion.2
  289.6 0.6 fusion.48
  290.2 3.7 dynamic-slice_dynamic-update-slice_fusion.2
  294.0 0.6 fusion.48
  294.6 3.7 dynamic-slice_dynamic-update-slice_fusion.2
  298.4 0.6 fusion.48
  298.9 3.7 dynamic-slice_dynamic-update-slice_fusion.2
  303.3 3.7 dynamic-slice_dynamic-update-slice_fusion.2
  307.7 3.7 dynamic-slice_dynamic-update-slice_fusion.2
  312.0 3.7 dynamic-slice_dynamic-update-slice_fusion.2
  316.4 3.7 dynamic-slice_dynamic-update-slice_fusion.2
  320.8 3.7 dynamic-slice_dynamic-update-slice_fusion.2
  325.2 3.7 dynamic-slice_dynamic-update-slice_fusion.2
  329.5 3.7 dynamic-slice_dynamic-update-slice_fusion.2
  333.9 3.7 dynamic-slice_dynamic-update-slice_fusion.2
  338.3 3.7 dynamic-slice_dynamic-update-slice_fusion.2
  342.6 3.7 dynamic-slice_dynamic-update-slice_fusion.2
  347.0 3.7 dynamic-slice_dynamic-update-slice_fusion.2
  350.7 4.4 multiply_convert_fusion
  355.1 319.5 %reduce-scatter.2.cloned.1.call-done = f32[16,64,512]{2,1,0:T(8,128)} async-done(((f32[16,512,512]{2,1,0:T(8,128)}), f32[16,64,512]{2,1,0:T(8,128)}) %reduce-scatter.2.cloned.1.call-update) | async-done | bytes 2097168 | tf_op jit(solution)/shard_map/reduce_scatter | solution.py:66
  674.6 4.9 fusion.9
  (52 shorter events, 7.8 us)
Async XLA Ops:
  6.5 6.6 copy-start
  6.5 9.2 %copy-start.4 = (s32[16]{0:T(128)S(1)}, s32[16]{0:T(128)}, u32[]{:S(2)}) copy-start(s32[16]{0:T(128)} %param.9) | copy-start | bytes 196
  6.5 125.7 %all-gather.2.cloned.1.call-start = ((), (), s32[]{:S(2)}) async-start(), calls=%async_computation.1 | async-start | bytes 20054016 | tf_op jit(solution)/shard_map/all_gather | solution.py:56
  7.3 667.3 %reduce-scatter.2.cloned.1.call-start = ((), (), s32[]{:S(2)}) async-start(), calls=%async_computation.2 | async-start | bytes 18874368 | tf_op jit(solution)/shard_map/reduce_scatter | solution.py:66
  12.4 2.4 copy-start.3
  174.4 8.1 %copy-start.2 = (bf16[16,576,256]{1,0,2:T(8,128)(2,1)S(1)}, bf16[16,576,256]{1,0,2:T(8,128)(2,1)}, u32[]{:S(2)}) copy-start(bf16[16,576,256]{1,0,2:T(8,128)(2,1)} %copy.6) | copy-start | bytes 14155780
  182.5 11.2 %slice-start = ((s8[5242880]{0:T(1024)(128)(4,1)}), s8[4194304]{0:T(1024)(128)(4,1)S(1)}, s32[]{:S(2)}) async-start(s8[5242880]{0:T(1024)(128)(4,1)} %bitcast.41), calls=%async_computation.3 | async-start | bytes 8388608
  188.1 5.6 slice-start.1
  350.7 328.8 %copy-start.1 = (bf16[16,16,1024]{2,1,0:T(8,128)(2,1)S(1)}, bf16[16,16,1024]{2,1,0:T(8,128)(2,1)}, u32[]{:S(2)}) copy-start(bf16[16,16,1024]{2,1,0:T(8,128)(2,1)} %param.5) | copy-start | bytes 1572868
Sparse Core Ops, SparseCore 0:
  9.8 122.3 all-gather.1
  350.8 323.7 reduce-scatter.1
where the time goes:
time: 688 us; the launch traced here: 686 us
  waiting for transfers between devices  437 us (64%)
  local copies, waits for them, and re-layouts  142 us (21%)
  other arithmetic  48.1 us (7%)
  matrix products  46.3 us (7%)
  between operations  13.5 us (2%)
    reduce_scatter x1, waiting for transfers between devices, per_device(): lax.psum_scatter(windows, 'pt', scatter_dimension=1, tiled=True)  319 us
    all_gather x1, waiting for transfers between devices, per_device(): lax.all_gather(point_store, 'shot', axis=0, tiled=True)  116 us
    gather x48, local copies, waits for them, and re-layouts  69.8 us
    slice x2, local copies, waits for them, and re-layouts, complex_product(): right_real = right_part[..., :bins]  17.3 us
    dot_general x1, matrix products, per_device(): jnp.dot(lax.all_gather(point_store, 'shot', axis=0, tiled=True), forward,...  16 us
    concatenate x1, other arithmetic, complex_product(): return jnp.concatenate([real_part, imag_part], axis=-1)  15 us
  transfers between devices with their start and end apart: 2, of which 2 were waited for; matrix products, arithmetic and copies ran while one was open for 2% of the time, Pallas kernels for 0%

commit v1 on v0

v1 whole, which is shorter than its diff:
```python
import functools
import math

import jax
import jax.numpy as jnp
import numpy as np
from jax import lax
from jax.experimental import pallas as pl
from jax.experimental.pallas import tpu as pltpu
from jax.sharding import PartitionSpec as P


NT = 1024
NF = 256
GRID = 576
SPREAD = 512
DEV = 128
ROWS = 4
NS = 16
NPT = 8
SHARE = 64
VMEM = 56 * 1024 * 1024


def band_tables():
    phase = (np.arange(NT)[:, None] * np.arange(NF)[None, :]) % NT
    angle = phase.astype(np.float32) * np.float32(2.0 * math.pi / NT)
    cosine = np.cos(angle).T
    sine = np.sin(angle).T
    weights = np.where(np.arange(NF) == 0, 1.0, 2.0).astype(np.float32)[:, None] / np.float32(NT)
    forward = np.stack([cosine[0::2], -sine[0::2], cosine[1::2], -sine[1::2]])
    wc, ws = weights * cosine, -weights * sine
    inverse = np.stack([wc[0::2], ws[0::2], wc[1::2], ws[1::2]])
    forward = jnp.asarray(forward.reshape(ROWS * DEV, NT), jnp.bfloat16)
    inverse = jnp.asarray(inverse.reshape(ROWS * DEV, NT), jnp.bfloat16)
    return forward, inverse


def iota(shape, dim):
    return lax.broadcasted_iota(jnp.int32, shape, dim)


def dot_nt(left, right):
    return lax.dot_general(left, right, (((1,), (1,)), ((), ())), preferred_element_type=jnp.float32)


def dot_nn(left, right):
    return jnp.dot(left, right, preferred_element_type=jnp.float32)


def forward_kernel(shot_ref, store_ref, slot_ref, mask_ref, start_ref, table_ref, out_ref, rows):
    f32, b16 = jnp.float32, jnp.bfloat16
    wide = NS * NS
    spread = (iota((NS, wide), 1) % NS == iota((NS, wide), 0)).astype(f32).astype(b16)
    owner = lax.shift_right_logical(slot_ref[...], 3).astype(f32).astype(b16)
    owner = dot_nn(jnp.broadcast_to(owner, (NS, NS)), spread)[0:1].astype(jnp.int32)
    taper = dot_nn(mask_ref[...].astype(f32).astype(b16), spread)
    taper = jnp.where(iota((NS, wide), 1) // NS == iota((NS, wide), 0), taper, 0.0)
    taper = jnp.sum(taper, axis=0, keepdims=True)
    r, l = iota((wide, wide), 0), iota((wide, wide), 1)
    order = jnp.where((r // NS == l // NS) & (owner == r % NS), taper, 0.0).astype(b16)
    table = table_ref[...]
    spectra = dot_nt(table, shot_ref[...].reshape(wide, NT)).astype(b16)
    ordered = dot_nt(spectra, order)
    gathers = dot_nt(table, store_ref[0, 0:SPREAD])
    tail = jnp.concatenate([store_ref[0, SPREAD:GRID], jnp.zeros((64, NT), b16)], axis=0)
    tail = dot_nt(table, tail)
    pick = (iota((NS, 128), 1) - 64 == iota((NS, 128), 0)).astype(f32).astype(b16)
    start = start_ref[...].astype(f32).astype(b16)
    start = dot_nn(jnp.broadcast_to(start, (NS, NS)), pick)[0:1]
    tail = tail + start
    for block, value in ((0, ordered), (2, gathers), (6, tail)):
        for n in range(value.shape[1] // 128):
            for c in range(ROWS):
                rows[pl.ds(4 * (block + n) + c, DEV, 32), :] = value[c * DEV : (c + 1) * DEV, 128 * n : 128 * (n + 1)]
    for c in range(ROWS):
        rows[pl.ds(28 + c, DEV, 32), :] = jnp.zeros((DEV, 128), f32)
    out_ref[...] = rows[...].astype(b16).reshape(DEV, 32, 128)


def product_kernel(in_ref, out_ref, rows, left, prod, wins):
    f32, b16 = jnp.float32, jnp.bfloat16
    rows[...] = in_ref[...].reshape(DEV * 32, 128).astype(f32)

    def piece(block, c):
        return rows[pl.ds(4 * block + c, DEV, 32), :]

    a, b = iota((128, 1024), 0), iota((128, 1024), 1)
    tile = ((a // 16 == b // 128) & (a % 16 == (b % 128) // 8)).astype(f32).astype(b16)
    halves = []
    keep = iota((512, 1024), 0) % 8 == iota((512, 1024), 1) % 8
    fold = (iota((64, 512), 0) == iota((64, 512), 1) // 8).astype(f32).astype(b16)
    for half in range(2):
        arrived = jnp.concatenate([piece(half, c) for c in range(ROWS)], axis=0).astype(b16)
        spread = dot_nn(arrived, tile)
        spread = jnp.where(keep, spread, 0.0).astype(b16)
        halves.append(dot_nn(fold, spread))
    for f in range(2):
        for s in range(NS):
            part = halves[s // 8][:, (s % 8) * 128 : (s % 8 + 1) * 128]
            re = part[(2 * f) * NS : (2 * f + 1) * NS]
            im = part[(2 * f + 1) * NS : (2 * f + 2) * NS]
            left[s * NS : (s + 1) * NS, 0:128] = re.astype(b16)
            left[s * NS : (s + 1) * NS, 128:256] = (-im).astype(b16)
            left[256 + s * NS : 256 + (s + 1) * NS, 0:128] = im.astype(b16)
            left[256 + s * NS : 256 + (s + 1) * NS, 128:256] = re.astype(b16)
        for n in range(5):
            right = jnp.concatenate([piece(2 + n, 2 * f), piece(2 + n, 2 * f + 1)], axis=0).astype(b16)
            prod[f * 512 : (f + 1) * 512, 128 * n : 128 * (n + 1)] = dot_nn(left[...], right)
    first = rows[pl.ds(24, NS, 32 * NPT), :][:, 64:80]
    lane = iota((NS, 128), 1)
    low = lane < 64
    for pair in range(NS // 2):
        begin = [
            jnp.broadcast_to(first[:, 2 * pair + e : 2 * pair + e + 1], (NS, 128)).astype(jnp.int32) for e in range(2)
        ]
        at = [lane + begin[0], lane + begin[1] + 64]
        index = [x & 127 for x in at]
        other = [(x + 64) & 127 for x in at]
        here = [lane + begin[0] + 64 < 128, lane + begin[1] < 128]
        for c in range(ROWS):
            base = c * 256 + 2 * pair * NS
            ahead = [None, None]
            for v in range(4, -1, -1):
                even, odd = [], []
                for e in range(2):
                    src = prod[base + e * NS : base + (e + 1) * NS, 128 * v : 128 * (v + 1)]
                    turned = jnp.take_along_axis(src, other[e], axis=1)
                    if v < 4:
                        even.append(jnp.take_along_axis(src, index[e], axis=1))
                        odd.append(jnp.where(here[e], turned, ahead[e]))
                    ahead[e] = turned
                if v < 4:
                    slot = c * 8 + pair
                    wins[pl.ds(2 * v * 32 + slot, NS, 256), :] = jnp.where(low, even[0], even[1])
                    wins[pl.ds((2 * v + 1) * 32 + slot, NS, 256), :] = jnp.where(low, odd[0], odd[1])
    out_ref[...] = wins[...].astype(b16).reshape(DEV, 32, 128)


def inverse_kernel(in_ref, table_ref, out_ref, rows):
    step = pl.program_id(0)

    @pl.when(step == 0)
    def _():
        rows[...] = in_ref[...].reshape(DEV * 32, 128).astype(jnp.float32)

    parts = [rows[pl.ds(c * 8 + step, DEV, 32), :].T for c in range(ROWS)]
    left = jnp.concatenate(parts, axis=1).astype(jnp.bfloat16)
    out_ref[...] = dot_nn(left, table_ref[...]).reshape(2, SHARE, NT)


def per_device(shot_data, point_store, point_slot, taper_mask, recv_start):
    forward, inverse = band_tables()
    params = pltpu.CompilerParams(vmem_limit_bytes=VMEM)
    sent = pl.pallas_call(
        forward_kernel,
        out_shape=jax.ShapeDtypeStruct((DEV, 32, 128), jnp.bfloat16),
        scratch_shapes=[pltpu.VMEM((DEV * 32, 128), jnp.float32)],
        compiler_params=params,
        name="forward",
    )(shot_data, point_store, point_slot.reshape(1, NS), taper_mask, recv_start.reshape(1, NS), forward)
    got = lax.all_to_all(sent, ("shot", "pt"), 0, 0, tiled=True)
    windows = pl.pallas_call(
        product_kernel,
        out_shape=jax.ShapeDtypeStruct((DEV, 32, 128), jnp.bfloat16),
        scratch_shapes=[
            pltpu.VMEM((DEV * 32, 128), jnp.float32),
            pltpu.VMEM((512, 256), jnp.bfloat16),
            pltpu.VMEM((1024, 640), jnp.float32),
            pltpu.VMEM((DEV * 32, 128), jnp.float32),
        ],
        compiler_params=params,
        name="product",
    )(got)
    back = lax.all_to_all(windows, ("shot", "pt"), 0, 0, tiled=True)
    return pl.pallas_call(
        inverse_kernel,
        grid=(NS // 2,),
        in_specs=[
            pl.BlockSpec((DEV, 32, 128), lambda i: (0, 0, 0)),
            pl.BlockSpec((ROWS * DEV, NT), lambda i: (0, 0)),
        ],
        out_specs=pl.BlockSpec((2, SHARE, NT), lambda i: (i, 0, 0)),
        out_shape=jax.ShapeDtypeStruct((NS, SHARE, NT), jnp.float32),
        scratch_shapes=[pltpu.VMEM((DEV * 32, 128), jnp.float32)],
        compiler_params=params,
        name="inverse",
    )(back, inverse)


def solution(mesh):
    placed = (
        P("shot", "pt", None),
        P(("shot", "pt"), None, None),
        P("pt"),
        P("shot", "pt"),
        P("shot"),
    )
    return jax.shard_map(
        per_device, mesh=mesh, in_specs=placed, out_specs=P("shot", "pt", None), check_vma=False
    )
```

time: 688 us -> 77.1 us (0.11)
  waiting for transfers between devices: 437 us -> 0 us
  local copies, waits for them, and re-layouts: 142 us -> 0 us
  blocking collectives: 0 us -> 55.9 us
  other arithmetic: 48.1 us -> 0 us
  matrix products: 46.3 us -> 0 us
  Pallas kernels: 0 us -> 20.9 us
  between operations: 13.5 us -> 0.01 us
    reduce_scatter x1 -> x0, waiting for transfers between devices: 319 us -> none  [per_device(): lax.psum_scatter(windows, 'pt', scatter_dimension=1, tiled=True)]
    all_gather x1 -> x0, waiting for transfers between devices: 116 us -> none  [per_device(): lax.all_gather(point_store, 'shot', axis=0, tiled=True)]
    gather x48 -> x0, local copies, waits for them, and re-layouts: 69.8 us -> none
    all_to_all x0 -> x2, blocking collectives: none -> 55.9 us  [the longest x1 31 us: per_device(): got = lax.all_to_all(sent, ('shot', 'pt'), 0, 0, tiled=True)]
    dot_general x7 -> x0, matrix products: 46.3 us -> none  [the longest x1 16 us: per_device(): jnp.dot(lax.all_gather(point_store, 'shot', axis=0, tiled=True), forward,...]
    dot_general x4 -> x0, local copies, waits for them, and re-layouts: 43.6 us -> none  [the longest x1 10.9 us: complex_product(): jnp.einsum('skf,krf->srf', left_real, right_imag, preferred_element_type=...]
    slice x6 -> x0, local copies, waits for them, and re-layouts: 28.2 us -> none  [the longest x2 17.3 us: complex_product(): right_real = right_part[..., :bins]]
    pallas_call x0 -> x3, Pallas kernels: none -> 20.9 us  [the longest x1 8.07 us: per_device(): pl.pallas_call(product_kernel, out_shape=jax.ShapeDtypeStruct((DEV, 32, 1...]
  transfers between devices with their start and end apart: 2 -> 0, of which waited for: 2 -> 0; matrix products, arithmetic and copies ran while one was open for 2% -> 0% of each run, Pallas kernels for 0% -> 0%
where the time goes in v1:
time: 77.1 us; the launch traced here: 76.8 us
  blocking collectives  55.9 us (73%)
  Pallas kernels  20.9 us (27%)
    all_to_all x1, blocking collectives, per_device(): got = lax.all_to_all(sent, ('shot', 'pt'), 0, 0, tiled=True)  31 us
    all_to_all x1, blocking collectives, per_device(): back = lax.all_to_all(windows, ('shot', 'pt'), 0, 0, tiled=True)  24.9 us
    pallas_call x1, Pallas kernels, per_device(): pl.pallas_call(product_kernel, out_shape=jax.ShapeDtypeStruct((DEV, 32, 1...  8.07 us
    pallas_call x1, Pallas kernels, per_device(): pl.pallas_call(inverse_kernel, grid=(NS // 2,), in_specs=[pl.BlockSpec((D...  7.07 us
    pallas_call x1, Pallas kernels, per_device(): pl.pallas_call(forward_kernel, out_shape=jax.ShapeDtypeStruct((DEV, 32, 1...  5.77 us

profile of v1, /device:TPU:1, one launch (start us, length us, event | category | flops | bytes accessed | tf_op | source)
XLA Modules:
  0.0 76.8 jit_solution(964697394815657766)
XLA Ops:
  0.0 5.8 %forward.1 = bf16[128,32,128]{2,1,0:T(8,128)(2,1)} custom-call(bf16[16,16,1024]{2,1,0:T(8,128)(2,1)} %shot_ref.1, bf16[1,576,1024]{2,1,0:T(8,128)(2,1)} %store_ref.1, s32[1,16]{1,0:T(1,128)} %bitcast.2, s32[16,16]{1,0:T(8,128)} %mask_ref.1, s32[1,16]{1,0:T(1,128)} %bitcast.3, bf16[512,1024]{1,0:T(8,128)(2,1)} %constant.4.clone.table_ref), custom_call_target="tpu_custom_call" | custom-call | tf_op jit(solution)/shard_map/forward/pallas_call | solution.py:155
  5.8 31.0 %all_to_all.10.in_ref = bf16[128,32,128]{2,1,0:T(8,128)(2,1)} all-to-all(bf16[128,32,128]{2,1,0:T(8,128)(2,1)} %forward.1), channel_id=1, replica_groups=mesh['shot'=16,'pt'=8] {'shot','pt'}, dimensions={0} | all-to-all | bytes 2097152 | tf_op jit(solution)/shard_map/all_to_all | solution.py:162
  36.7 8.1 %product.1 = bf16[128,32,128]{2,1,0:T(8,128)(2,1)} custom-call(bf16[128,32,128]{2,1,0:T(8,128)(2,1)} %all_to_all.10.in_ref), custom_call_target="tpu_custom_call" | custom-call | tf_op jit(solution)/shard_map/product/pallas_call | solution.py:163
  44.8 24.9 %all_to_all.11.in_ref = bf16[128,32,128]{2,1,0:T(8,128)(2,1)} all-to-all(bf16[128,32,128]{2,1,0:T(8,128)(2,1)} %product.1), channel_id=1, replica_groups=mesh['shot'=16,'pt'=8] {'shot','pt'}, dimensions={0} | all-to-all | bytes 2097152 | tf_op jit(solution)/shard_map/all_to_all | solution.py:175
  69.7 7.1 %inverse.1 = f32[16,64,1024]{2,1,0:T(8,128)} custom-call(bf16[128,32,128]{2,1,0:T(8,128)(2,1)} %all_to_all.11.in_ref, bf16[512,1024]{1,0:T(8,128)(2,1)} %constant.5.clone.table_ref), custom_call_target="tpu_custom_call" | custom-call | tf_op jit(solution)/shard_map/inverse/pallas_call | solution.py:176
